TPU v7x, 256 devices: a whole 4x4x8 slice. The times are simulated.
256 devices in a mesh: zslab: 8 (over y, x_lo), tile: 32 (over x_hi, z, core).
Axes of the slice: x: 4 (x_hi: 2, x_lo: 2; x = x_hi * 2 + x_lo), y: 4, z: 8, core: 2. Of those that a mesh axis runs over, the one named last changes fastest.
Arguments:
- estimate: float32 [128, 1024, 128], P('zslab', 'tile'), may hold values from 0.5 to 1.5
- view_data: float32 [6, 128, 1024, 128], P(None, 'zslab', 'tile'), may hold values from 0.2 to 3
- psf: float32 [6, 3, 31], replicated, may hold values from 0.05 to 1
- shifts: int32 [6], replicated, may hold values from -16 to 16, as said below
- extents: int32 [6, 2], replicated, may hold values from 0 to 128, as said below
Outputs:
- restored: float32 [128, 1024, 128], P('zslab', 'tile')
Inputs may be any that keep to these rules, and one draw needn't show every extreme that they name: `shifts`: each view's x-offset lies within 16 cells; some view is offset by exactly 16 and some by exactly -16. extents[v, 0] < extents[v, 1]; every z-plane lies in the extent of at least one view.
All inputs are finite; a program needn't handle non-finite values.
Results may differ from a plain program's by a relative error of at most 0.0003.
Values sent between devices are 32-bit elements; how exact they have to be, the bound alone decides.
A program may use at most 64 MiB of HBM per device.

v0:
```python
import functools

import jax
import jax.numpy as jnp
from jax import lax
from jax.experimental import pallas as pl
from jax.experimental.pallas import tpu as pltpu
from jax.sharding import PartitionSpec as P

MESH = pl.DeviceIdType.MESH
V, TAPS, ITERS = 6, 31, 2
H = TAPS // 2
W = 16
D, R, C = 16, 32, 128
DE, RE = D + 2 * W, R + 2 * W
F32, BF16 = jnp.float32, jnp.bfloat16


def halves(x):
    hi = x.astype(BF16)
    return hi, (x - hi.astype(F32)).astype(BF16)


def stacked(x):
    hi, lo = halves(x)
    return jnp.concatenate([hi, lo, hi], axis=0)


def dot(a, b):
    return jnp.dot(a, b, preferred_element_type=F32)


def band(psf, v, a, offset):
    def tap(t, carry):
        total, weight = carry
        p = psf[v, a, t]
        return jnp.where(offset == t, p, total), weight + p

    zeros = jnp.zeros(offset.shape, F32)
    total, weight = lax.fori_loop(0, TAPS, tap, (zeros, zeros))
    return total / weight


def iota(shape, dim):
    return lax.broadcasted_iota(jnp.int32, shape, dim)


def high_low(value, part):
    hi, lo = halves(value)
    return jnp.where(part == 2, lo.astype(F32), hi.astype(F32)).astype(BF16)


def kernel(
    nz, nt, est, view, psf, shifts, extents, out,
    raw, near, ext, zbuf, xbuf, rbuf, back, got_x, got_z,
    kz, kzt, kx, kxt, ky, kyt, send, recv, local,
):
    zs, ti = lax.axis_index("zslab"), lax.axis_index("tile")
    place = {"zslab": (zs, nz), "tile": (ti, nt)}

    def there(axis, step):
        me, count = place[axis]
        return me + step < count if step > 0 else me + step >= 0

    class Sent:
        def __init__(self, number, src, dst, axis, step):
            self.axis, self.step = axis, step
            self.copy = pltpu.make_async_remote_copy(
                src_ref=src, dst_ref=dst, send_sem=send.at[number], recv_sem=recv.at[number],
                device_id={axis: place[axis][0] + step}, device_id_type=MESH,
            )

        def start(self):
            pl.when(there(self.axis, self.step))(self.copy.start)

        def sent(self):
            pl.when(there(self.axis, self.step))(self.copy.wait_send)

        def arrived(self):
            pl.when(there(self.axis, -self.step))(self.copy.wait_recv)

    own_est = pltpu.make_async_copy(est, raw, local.at[0])
    own_est.start()
    own_view = pltpu.make_async_copy(view, near.at[:, W : W + R], local.at[1])
    own_view.start()

    ext[...] = jnp.zeros(ext.shape, F32)
    got_x[...] = jnp.zeros(got_x.shape, F32)
    got_z[...] = jnp.zeros(got_z.shape, F32)
    near[:, 0:W] = jnp.zeros((V * D, W, C), F32)
    near[:, W + R :] = jnp.zeros((V * D, W, C), F32)
    own_est.wait()
    for x in range(R):
        ext[W + x, W : W + D] = raw[pl.ds(x, D, stride=R)]

    barrier = pltpu.get_barrier_semaphore()
    beside = [(axis, step) for axis in ("zslab", "tile") for step in (-1, 1)]
    for axis, step in beside:

        @pl.when(there(axis, step))
        def _():
            pl.semaphore_signal(
                barrier, inc=1, device_id={axis: place[axis][0] + step}, device_id_type=MESH
            )

    pl.semaphore_wait(barrier, sum(there(axis, step).astype(jnp.int32) for axis, step in beside))

    own_x, own_z = slice(W, W + R), slice(W, W + D)
    planes = [own_z, slice(0, W), slice(W + D, DE)]
    views = [
        Sent(0, view.at[:, 0:W], near.at[:, W + R : RE], "tile", -1),
        Sent(1, view.at[:, R - W : R], near.at[:, 0:W], "tile", 1),
    ]
    est_z = [
        Sent(2, ext.at[own_x, own_z], ext.at[own_x, W + D : DE], "zslab", -1),
        Sent(3, ext.at[own_x, own_z], ext.at[own_x, 0:W], "zslab", 1),
    ]
    est_x = [
        [
            Sent(4 + 2 * k, ext.at[W : W + H, p], ext.at[W + R : W + R + H, p], "tile", -1),
            Sent(5 + 2 * k, ext.at[W + R - H : W + R, p], ext.at[1 : 1 + H, p], "tile", 1),
        ]
        for k, p in enumerate(planes)
    ]
    back_x = [
        [
            Sent(10 + 2 * k, back.at[1 : 1 + H, p], got_x.at[1, :, p], "tile", -1),
            Sent(11 + 2 * k, back.at[W + R : W + R + H, p], got_x.at[0, :, p], "tile", 1),
        ]
        for k, p in enumerate(planes)
    ]
    back_z = [
        Sent(16, back.at[own_x, 0:W], got_z.at[1], "zslab", -1),
        Sent(17, back.at[own_x, W + D : DE], got_z.at[0], "zslab", 1),
    ]

    def build():
        def one(v, carry):
            row, col = iota((D, 3 * DE), 0), iota((D, 3 * DE), 1)
            part = (col >= DE).astype(jnp.int32) + (col >= 2 * DE).astype(jnp.int32)
            kz[pl.ds(pl.multiple_of(v * D, D), D)] = high_low(
                band(psf, v, 2, col - part * DE - row - 1), part
            )
            row, col = iota((R, 3 * RE), 0), iota((R, 3 * RE), 1)
            kx[v] = high_low(band(psf, v, 0, (col & (RE - 1)) - row - 1), col // RE)
            row, col = iota((RE, 3 * R), 0), iota((RE, 3 * R), 1)
            kxt[v] = high_low(band(psf, v, 0, row - (col & (R - 1)) - 1), col // R)
            row, col = iota((C, C), 0), iota((C, C), 1)
            for mat, sign in ((ky, 1), (kyt, -1)):
                hi, lo = halves(band(psf, v, 1, sign * (row - col) + H))
                mat[v, 0:C, 0:C] = hi
                mat[v, 0:C, C:] = lo
                mat[v, C:, 0:C] = hi
                mat[v, C:, C:] = jnp.zeros((C, C), BF16)
            return carry

        lax.fori_loop(0, V, one, 0)
        shape = (DE, 3 * V * D)
        row, col = iota(shape, 0), iota(shape, 1)
        part = (col >= V * D).astype(jnp.int32) + (col >= 2 * V * D).astype(jnp.int32)
        inner = col - part * V * D

        def own(v, total):
            value = band(psf, v, 2, row - (inner & (D - 1)) - 1)
            return jnp.where(inner // D == v, value, total)

        kzt[...] = high_low(lax.fori_loop(0, V, own, jnp.zeros(shape, F32)), part)

    def along_z(i, carry):
        x = 2 * i
        o = dot(kz[...], stacked(jnp.concatenate([ext[x], ext[x + 1]], axis=1)))
        for v in range(V):
            for k in range(2):
                at = pl.multiple_of((x + k) * D, D)
                zbuf[v, pl.ds(at, D)] = o[v * D : (v + 1) * D, k * C : (k + 1) * C]
        return carry

    def one_view(v, carry):
        for i in range(0, D, 2):
            both = [zbuf[v, pl.ds(i + k, RE, stride=D)] for k in range(2)]
            o = dot(kx[v], stacked(jnp.concatenate(both, axis=1)))
            xbuf[i * R : (i + 1) * R] = o[:, :C]
            xbuf[(i + 1) * R : (i + 2) * R] = o[:, C:]
        o = dot(jnp.concatenate(halves(xbuf[...]), axis=1), ky[v])
        blurred = o[:, :C] + o[:, C:]
        start = W + shifts[v]
        for z in range(D):
            plane = zs * D + z
            inside = jnp.where((plane >= extents[v, 0]) & (plane < extents[v, 1]), 1.0, 0.0)
            data = near[v * D + z, pl.ds(start, R)]
            xbuf[z * R : (z + 1) * R] = inside * data / blurred[z * R : (z + 1) * R]
        o = dot(jnp.concatenate(halves(xbuf[...]), axis=1), kyt[v])
        xbuf[...] = o[:, :C] + o[:, C:]
        for i in range(0, D, 2):
            both = [xbuf[(i + k) * R : (i + k + 1) * R] for k in range(2)]
            o = dot(kxt[v], stacked(jnp.concatenate(both, axis=1)))
            for k in range(2):
                rbuf[pl.ds(v * D + i + k, RE, stride=V * D)] = o[:, k * C : (k + 1) * C]
        return carry

    def along_z_back(i, carry):
        x = 2 * i
        both = [rbuf[pl.ds(pl.multiple_of((x + k) * V * D, V * D), V * D)] for k in range(2)]
        o = dot(kzt[...], stacked(jnp.concatenate(both, axis=1)))
        back[x] = o[:, :C]
        back[x + 1] = o[:, C:]
        return carry

    depth = zs * D + iota((D, C), 0)
    count = jnp.zeros((D, C), F32)
    for v in range(V):
        held = (depth >= extents[v, 0]) & (depth < extents[v, 1])
        count = count + jnp.where(held, 1.0, 0.0)

    for step in range(ITERS):
        for copy in est_z + est_x[0]:
            copy.start()
        if step == 0:
            for copy in views:
                copy.start()
            build()
        est_z[0].arrived()
        for copy in est_x[2]:
            copy.start()
        est_z[1].arrived()
        for copy in est_x[1]:
            copy.start()
        for pair in est_x:
            for copy in pair:
                copy.arrived()
        lax.fori_loop(0, RE // 2, along_z, 0, unroll=2)
        if step == 0:
            own_view.wait()
            for copy in views:
                copy.arrived()
        lax.fori_loop(0, V, one_view, 0)
        lax.fori_loop(0, RE // 2, along_z_back, 0, unroll=2)
        for pair in (back_x[1], back_x[2], back_x[0]):
            for copy in pair:
                copy.start()
        for copy in est_z:
            copy.sent()
        for pair in est_x:
            for copy in pair:
                copy.sent()
        for k in (1, 2, 0):
            for copy in back_x[k]:
                copy.arrived()
            p = planes[k]
            back[W : W + H, p] += got_x[0, :, p]
            back[W + R - H : W + R, p] += got_x[1, :, p]
            if k > 0:
                back_z[k - 1].start()
        for copy in back_z:
            copy.arrived()
        for x in range(R):
            total = back[W + x, own_z] + got_z[0, x] + got_z[1, x]
            updated = ext[W + x, own_z] * total / count
            if step < ITERS - 1:
                ext[W + x, own_z] = updated
            else:
                out[pl.ds(x, D, stride=R)] = updated
        for pair in back_x + [back_z]:
            for copy in pair:
                copy.sent()
    for copy in views:
        copy.sent()


def solution(mesh):
    nz, nt = mesh.shape["zslab"], mesh.shape["tile"]

    def per_device(estimate, view_data, psf, shifts, extents):
        flat = pl.pallas_call(
            functools.partial(kernel, nz, nt),
            out_shape=jax.ShapeDtypeStruct((D * R, C), F32),
            in_specs=[pl.BlockSpec(memory_space=pl.ANY)] * 2
            + [pl.BlockSpec(memory_space=pltpu.SMEM)] * 3,
            out_specs=pl.BlockSpec(memory_space=pltpu.VMEM),
            scratch_shapes=[
                pltpu.VMEM((D * R, C), F32),
                pltpu.VMEM((V * D, RE, C), F32),
                pltpu.VMEM((RE, DE, C), F32),
                pltpu.VMEM((V, RE * D, C), F32),
                pltpu.VMEM((D * R, C), F32),
                pltpu.VMEM((RE * V * D, C), F32),
                pltpu.VMEM((RE, DE, C), F32),
                pltpu.VMEM((2, H, DE, C), F32),
                pltpu.VMEM((2, R, D, C), F32),
                pltpu.VMEM((V * D, 3 * DE), BF16),
                pltpu.VMEM((DE, 3 * V * D), BF16),
                pltpu.VMEM((V, R, 3 * RE), BF16),
                pltpu.VMEM((V, RE, 3 * R), BF16),
                pltpu.VMEM((V, 2 * C, 2 * C), BF16),
                pltpu.VMEM((V, 2 * C, 2 * C), BF16),
                pltpu.SemaphoreType.DMA((18,)),
                pltpu.SemaphoreType.DMA((18,)),
                pltpu.SemaphoreType.DMA((2,)),
            ],
            compiler_params=pltpu.CompilerParams(
                collective_id=0, has_side_effects=True, vmem_limit_bytes=48 * 1024 * 1024
            ),
        )(
            estimate.reshape(D * R, C),
            view_data.reshape(V * D, R, C),
            psf,
            shifts,
            extents,
        )
        return flat.reshape(D, R, C)

    placed = (P("zslab", "tile", None), P(None, "zslab", "tile", None), P(), P(), P())
    return jax.shard_map(
        per_device, mesh=mesh, in_specs=placed, out_specs=P("zslab", "tile", None), check_vma=False
    )
```

profile of v0, /device:TPU:17, one launch (start us, length us, event | category | flops | bytes accessed | tf_op | source)
XLA Modules:
  0.0 107.4 jit_solution(13975872575822596068)
XLA Ops:
  0.0 0.8 copy.6.extents
  0.8 0.0 copy-start
  0.8 1.4 %copy-done = f32[6,16,32,128]{3,2,1,0:T(8,128)S(1)} copy-done((f32[6,16,32,128]{3,2,1,0:T(8,128)S(1)}, f32[6,16,32,128]{3,2,1,0:T(8,128)}, u32[]{:S(2)}) %copy-start) | copy-done | bytes 1572888
  2.2 0.0 copy-start.1
  2.2 0.9 copy-done.1
  3.1 0.0 copy-start.2
  3.1 0.7 copy-done.2
  3.8 0.0 copy-start.3
  3.8 0.7 copy-done.3
  4.5 102.2 %shard_map.55 = f32[512,128]{1,0:T(8,128)S(1)} custom-call(f32[512,128]{1,0:T(8,128)S(1)} %bitcast.5, f32[96,32,128]{2,1,0:T(8,128)S(1)} %bitcast.3, f32[6,3,31]{2,1,0:T(4,128)S(1)} %copy-done.2, s32[6]{0:T(128)S(1)} %copy-done.3, s32[6,2]{1,0:T(8,128)S(1)} %copy.6.extents), custom_call_target="tpu_custom_call" | custom-call | tf_op jit(solution)/shard_map/pallas_call | solution.py:274
  106.7 0.7 copy.8
Async XLA Ops:
  0.8 1.4 %copy-start = (f32[6,16,32,128]{3,2,1,0:T(8,128)S(1)}, f32[6,16,32,128]{3,2,1,0:T(8,128)}, u32[]{:S(2)}) copy-start(f32[6,16,32,128]{3,2,1,0:T(8,128)} %param.6) | copy-start | bytes 4718596
  2.2 0.9 copy-start.1
  3.1 0.7 copy-start.2
  3.8 0.7 copy-start.3
where the time goes:
time: 108 us; the launch traced here: 107 us
  Pallas kernels  102 us (94%)
  local copies, waits for them, and re-layouts  5.19 us (5%)
    pallas_call x1, Pallas kernels, per_device(): pl.pallas_call(functools.partial(kernel, nz, nt), out_shape=jax.ShapeDtyp...  102 us
    unnamed x10, local copies, waits for them, and re-layouts  5.19 us

commit v1 on v0

v1 whole, which is shorter than its diff:
```python
import functools

import jax
import jax.numpy as jnp
from jax import lax
from jax.experimental import pallas as pl
from jax.experimental.pallas import tpu as pltpu
from jax.sharding import PartitionSpec as P

MESH = pl.DeviceIdType.MESH
V, TAPS, ITERS = 6, 31, 2
H = TAPS // 2
W = 16
D, R, C = 16, 32, 128
DE, RE = D + 2 * W, R + 2 * W
N = 8
ORDER = (0, 24, 8, 16)
SEMS = 2 + 10 * len(ORDER)
F32, BF16 = jnp.float32, jnp.bfloat16


def halves(x):
    hi = x.astype(BF16)
    return hi, (x - hi.astype(F32)).astype(BF16)


def stacked(x):
    hi, lo = halves(x)
    return jnp.concatenate([hi, lo, hi], axis=0)


def dot(a, b):
    return jnp.dot(a, b, preferred_element_type=F32)


def split_part(value):
    hi, lo = halves(value)
    return hi.astype(F32), lo.astype(F32)


def iota(shape, dim):
    return lax.broadcasted_iota(jnp.int32, shape, dim)


def taps(psf, v, a):
    lane = iota((8, C), 1)
    forward = jnp.zeros((8, C), F32)
    reverse = jnp.zeros((8, C), F32)
    for t in range(TAPS):
        p = psf[v, a, t]
        forward = jnp.where(lane == t, p, forward)
        reverse = jnp.where(lane == TAPS - 1 - t, p, reverse)
    weight = jnp.sum(forward, axis=1, keepdims=True)
    return forward / weight, reverse / weight


def slanted(row, rows, first):
    whole = jnp.concatenate([row] * (rows // 8), axis=0)
    return pltpu.roll(whole, first % C, 1, stride=1, stride_axis=0)


def kernel(
    nz, nt, est, view, psf_in, shifts_in, extents_in, out,
    raw, near, ext, zbuf, xbuf, rbuf, back, got_x, got_y, got_n,
    kz, kzt, kx, kxt, ky, kyt, psf, shifts, extents, send, recv, local,
):
    zs, ti = lax.axis_index("zslab"), lax.axis_index("tile")
    odd = lax.rem(zs, 2)
    mate, ahead, behind = zs + 1 - 2 * odd, zs + 2 - 4 * odd, zs - 2 + 4 * odd
    close = pl.multiple_of(2 * W * (1 - odd), W)
    far = pl.multiple_of(2 * W * odd, W)
    is_mate = mate < nz

    class Sent:
        def __init__(self, number, src, dst, axis, target, exists, comes):
            self.exists, self.comes = exists, comes
            self.copy = pltpu.make_async_remote_copy(
                src_ref=src, dst_ref=dst, send_sem=send.at[number], recv_sem=recv.at[number],
                device_id={axis: target}, device_id_type=MESH,
            )

        def start(self):
            pl.when(self.exists)(self.copy.start)

        def sent(self):
            pl.when(self.exists)(self.copy.wait_send)

        def arrived(self):
            pl.when(self.comes)(self.copy.wait_recv)

    is_ahead = (ahead >= 0) & (ahead < nz)
    is_behind = (behind >= 0) & (behind < nz)
    is_left, is_right = ti > 0, ti < nt - 1
    numbers = iter(range(SEMS))

    def to_mate(src, dst):
        return Sent(next(numbers), src, dst, "zslab", mate, is_mate, is_mate)

    def to_ahead(src, dst):
        return Sent(next(numbers), src, dst, "zslab", ahead, is_ahead, is_behind)

    def to_behind(src, dst):
        return Sent(next(numbers), src, dst, "zslab", behind, is_behind, is_ahead)

    def to_left(src, dst):
        return Sent(next(numbers), src, dst, "tile", ti - 1, is_left, is_right)

    def to_right(src, dst):
        return Sent(next(numbers), src, dst, "tile", ti + 1, is_right, is_left)

    reads = [
        pltpu.make_async_copy(src, dst, local.at[k])
        for k, (src, dst) in enumerate(
            [(est, raw), (view, near.at[:, W : W + R]), (psf_in, psf), (shifts_in, shifts), (extents_in, extents)]
        )
    ]
    for read in reads:
        read.start()

    ext[...] = jnp.zeros(ext.shape, F32)
    got_x[...] = jnp.zeros(got_x.shape, F32)
    got_y[...] = jnp.zeros(got_y.shape, F32)
    near[:, 0:W] = jnp.zeros((V * D, W, C), F32)
    near[:, W + R :] = jnp.zeros((V * D, W, C), F32)
    for x in range(RE):
        rbuf[pl.ds(x * C + V * D, C - V * D)] = jnp.zeros((C - V * D, C), F32)
    reads[0].wait()
    for x in range(R):
        ext[W + x, W : W + D] = raw[pl.ds(x, D, stride=R)]

    barrier = pltpu.get_barrier_semaphore()
    beside = [
        ("zslab", mate, is_mate), ("zslab", ahead, is_ahead), ("zslab", behind, is_behind),
        ("tile", ti - 1, is_left), ("tile", ti + 1, is_right),
    ]
    for axis, target, exists in beside:

        @pl.when(exists)
        def _(axis=axis, target=target):
            pl.semaphore_signal(barrier, inc=1, device_id={axis: target}, device_id_type=MESH)

    pl.semaphore_wait(barrier, sum(exists.astype(jnp.int32) for _, _, exists in beside))

    own_p, close_p, far_p = pl.ds(W, D), pl.ds(close, W), pl.ds(far, W)

    def rows_of(r):
        return slice(W + r, W + r + N)

    def est_tile(r, p):
        src = ext.at[rows_of(r), p]
        if r < W:
            return to_left(src, ext.at[W + R + r : W + R + r + N, p])
        return to_right(src, ext.at[r - W : r - W + N, p])

    def back_tile(r, p):
        dst = got_x.at[r : r + N, p]
        if r < W:
            return to_right(back.at[W + R + r : W + R + r + N, p], dst)
        return to_left(back.at[r - W : r - W + N, p], dst)

    views = [
        to_left(view.at[:, 0:W], near.at[:, W + R : RE]),
        to_right(view.at[:, R - W : R], near.at[:, 0:W]),
    ]
    est_mate = {r: to_mate(ext.at[rows_of(r), own_p], ext.at[rows_of(r), far_p]) for r in ORDER}
    est_ahead = {r: to_ahead(ext.at[rows_of(r), close_p], ext.at[rows_of(r), far_p]) for r in ORDER}
    est_own = {r: est_tile(r, own_p) for r in ORDER}
    est_close = {r: est_tile(r, close_p) for r in ORDER}
    est_far = {r: est_tile(r, far_p) for r in ORDER}
    back_far = {r: back_tile(r, far_p) for r in ORDER}
    back_close = {r: back_tile(r, close_p) for r in ORDER}
    back_own = {r: back_tile(r, own_p) for r in ORDER}
    back_behind = {r: to_behind(back.at[rows_of(r), far_p], got_y.at[r : r + N]) for r in ORDER}
    back_mate = {r: to_mate(back.at[rows_of(r), close_p], got_n.at[r : r + N]) for r in ORDER}
    est_sends = [est_mate, est_ahead, est_own, est_close, est_far]
    back_sends = [back_far, back_close, back_own, back_behind, back_mate]

    def build():
        lane = iota((C, C), 1)
        gap = iota((C, C), 0) - lane
        banded = (gap >= -H) & (gap <= H)

        def one(v, total):
            forward, reverse = taps(psf, v, 2)
            hi, lo = split_part(slanted(forward, D, 1))
            low = pltpu.roll(lo, 2 * DE, 1)
            at = pl.ds(pl.multiple_of(v * D, D), D)
            kz[at, 0:C] = (
                hi + pltpu.roll(hi, DE, 1) + jnp.where(lane[0:D] >= 2 * DE, low, 0.0)
            ).astype(BF16)
            kz[at, C:] = low[:, 0 : 3 * DE - C].astype(BF16)
            z_back = jnp.where(lane[0:DE] < D, slanted(reverse, DE, -TAPS), 0.0)
            forward, reverse = taps(psf, v, 0)
            hi, lo = split_part(slanted(forward, R, 1))
            kx[v, :, 0:C] = (hi + pltpu.roll(hi, RE, 1)).astype(BF16)
            kx[v, :, C:] = lo[:, 0:RE].astype(BF16)
            hi, lo = split_part(jnp.where(lane[0:RE] < R, slanted(reverse, RE, -TAPS), 0.0))
            kxt[v] = (hi + pltpu.roll(hi, R, 1) + pltpu.roll(lo, 2 * R, 1))[:, 0 : 3 * R].astype(BF16)
            forward, reverse = taps(psf, v, 1)
            for mat, row in ((ky, reverse), (kyt, forward)):
                hi, lo = halves(jnp.where(banded, slanted(row, C, -H), 0.0))
                mat[v, 0:C, 0:C] = hi
                mat[v, 0:C, C:] = lo
                mat[v, C:, 0:C] = hi
                mat[v, C:, C:] = jnp.zeros((C, C), BF16)
            return total + pltpu.roll(z_back, v * D, 1)

        hi, lo = halves(lax.fori_loop(0, V, one, jnp.zeros((DE, C), F32)))
        kzt[:, 0:C] = hi
        kzt[:, C : 2 * C] = hi
        kzt[:, 2 * C :] = lo

    def along_z(i, carry):
        x = 2 * i
        o = dot(kz[...], stacked(jnp.concatenate([ext[x], ext[x + 1]], axis=1)))
        for v in range(V):
            for k in range(2):
                at = pl.multiple_of((x + k) * D, D)
                zbuf[v, pl.ds(at, D)] = o[v * D : (v + 1) * D, k * C : (k + 1) * C]
        return carry

    def one_view(v, carry):
        for i in range(0, D, 2):
            both = [zbuf[v, pl.ds(i + k, RE, stride=D)] for k in range(2)]
            o = dot(kx[v], stacked(jnp.concatenate(both, axis=1)))
            xbuf[i * R : (i + 1) * R] = o[:, :C]
            xbuf[(i + 1) * R : (i + 2) * R] = o[:, C:]
        o = dot(jnp.concatenate(halves(xbuf[...]), axis=1), ky[v])
        blurred = o[:, :C] + o[:, C:]
        start = W + shifts[v]
        for z in range(D):
            plane = zs * D + z
            inside = jnp.where((plane >= extents[v, 0]) & (plane < extents[v, 1]), 1.0, 0.0)
            data = near[v * D + z, pl.ds(start, R)]
            xbuf[z * R : (z + 1) * R] = inside * data / blurred[z * R : (z + 1) * R]
        o = dot(jnp.concatenate(halves(xbuf[...]), axis=1), kyt[v])
        xbuf[...] = o[:, :C] + o[:, C:]
        for i in range(0, D, 2):
            both = [xbuf[(i + k) * R : (i + k + 1) * R] for k in range(2)]
            o = dot(kxt[v], stacked(jnp.concatenate(both, axis=1)))
            for k in range(2):
                rbuf[pl.ds(v * D + i + k, RE, stride=C)] = o[:, k * C : (k + 1) * C]
        return carry

    def along_z_back(i, carry):
        x = 2 * i
        both = [rbuf[pl.ds(pl.multiple_of((x + k) * C, C), C)] for k in range(2)]
        o = dot(kzt[...], stacked(jnp.concatenate(both, axis=1)))
        back[x] = o[:, :C]
        back[x + 1] = o[:, C:]
        return carry

    def over(body, first, rows):
        lax.fori_loop(first // 2, (first + rows) // 2, body, 0, unroll=2)

    for r in ORDER:
        est_mate[r].start()
        est_own[r].start()
    for copy in views:
        copy.start()
    for read in reads[2:]:
        read.wait()
    build()
    depth = zs * D + iota((D, C), 0)
    count = jnp.zeros((D, C), F32)
    for v in range(V):
        held = (depth >= extents[v, 0]) & (depth < extents[v, 1])
        count = count + jnp.where(held, 1.0, 0.0)

    for step in range(ITERS):
        for r in ORDER:
            est_mate[r].arrived()
            est_ahead[r].start()
            est_close[r].start()
        for r in ORDER:
            est_ahead[r].arrived()
            est_far[r].start()
            over(along_z, W + r, N)
        for r in ORDER:
            for group in (est_own, est_close, est_far):
                group[r].arrived()
            over(along_z, W + R + r if r < W else r - W, N)
        if step == 0:
            reads[1].wait()
            for copy in views:
                copy.arrived()
        lax.fori_loop(0, V, one_view, 0)
        for group in est_sends:
            for r in ORDER:
                group[r].sent()
        for r in ORDER:
            over(along_z_back, W + R + r if r < W else r - W, N)
            back_far[r].start()
        for group in (back_close, back_own):
            for r in ORDER:
                group[r].start()
        over(along_z_back, W, R)
        for r in ORDER:
            back_far[r].arrived()
            back[rows_of(r), far_p] += got_x[r : r + N, far_p]
            back_behind[r].start()
        for r in ORDER:
            back_close[r].arrived()
            back_behind[r].arrived()
            back[rows_of(r), close_p] += got_x[r : r + N, close_p] + got_y[r : r + N]
            back_mate[r].start()
        for r in ORDER:
            back_own[r].arrived()
            back_mate[r].arrived()
            for x in range(r, r + N):
                total = back[W + x, W : W + D] + got_x[x, W : W + D] + got_n[x]
                updated = ext[W + x, W : W + D] * total / count
                if step < ITERS - 1:
                    ext[W + x, W : W + D] = updated
                else:
                    out[pl.ds(x, D, stride=R)] = updated
            if step < ITERS - 1:
                est_mate[r].start()
                est_own[r].start()
        for group in back_sends:
            for r in ORDER:
                group[r].sent()
    for copy in views:
        copy.sent()


def solution(mesh):
    nz, nt = mesh.shape["zslab"], mesh.shape["tile"]

    def per_device(estimate, view_data, psf, shifts, extents):
        flat = pl.pallas_call(
            functools.partial(kernel, nz, nt),
            out_shape=jax.ShapeDtypeStruct((D * R, C), F32),
            in_specs=[pl.BlockSpec(memory_space=pl.ANY)] * 5,
            out_specs=pl.BlockSpec(memory_space=pltpu.VMEM),
            scratch_shapes=[
                pltpu.VMEM((D * R, C), F32),
                pltpu.VMEM((V * D, RE, C), F32),
                pltpu.VMEM((RE, DE, C), F32),
                pltpu.VMEM((V, RE * D, C), F32),
                pltpu.VMEM((D * R, C), F32),
                pltpu.VMEM((RE * C, C), F32),
                pltpu.VMEM((RE, DE, C), F32),
                pltpu.VMEM((R, DE, C), F32),
                pltpu.VMEM((R, D, C), F32),
                pltpu.VMEM((R, D, C), F32),
                pltpu.VMEM((V * D, 3 * DE), BF16),
                pltpu.VMEM((DE, 3 * C), BF16),
                pltpu.VMEM((V, R, 3 * RE), BF16),
                pltpu.VMEM((V, RE, 3 * R), BF16),
                pltpu.VMEM((V, 2 * C, 2 * C), BF16),
                pltpu.VMEM((V, 2 * C, 2 * C), BF16),
                pltpu.SMEM((V, 3, TAPS), F32),
                pltpu.SMEM((V,), jnp.int32),
                pltpu.SMEM((V, 2), jnp.int32),
                pltpu.SemaphoreType.DMA((SEMS,)),
                pltpu.SemaphoreType.DMA((SEMS,)),
                pltpu.SemaphoreType.DMA((5,)),
            ],
            compiler_params=pltpu.CompilerParams(
                collective_id=0, has_side_effects=True, vmem_limit_bytes=60 * 1024 * 1024
            ),
        )(
            estimate.reshape(D * R, C),
            view_data.reshape(V * D, R, C),
            psf,
            shifts,
            extents,
        )
        return flat.reshape(D, R, C)

    placed = (P("zslab", "tile", None), P(None, "zslab", "tile", None), P(), P(), P())
    return jax.shard_map(
        per_device, mesh=mesh, in_specs=placed, out_specs=P("zslab", "tile", None), check_vma=False
    )
```

time: 108 us -> 88 us (0.81)
  Pallas kernels: 102 us -> 84.8 us
  local copies, waits for them, and re-layouts: 5.19 us -> 3.02 us
    pallas_call x1, Pallas kernels: 102 us -> 84.8 us  [per_device(): pl.pallas_call(functools.partial(kernel, nz, nt), out_shape=jax.ShapeDtyp...]
    unnamed x10 -> x2, local copies, waits for them, and re-layouts: 5.19 us -> 3.02 us
where the time goes in v1:
time: 88 us; the launch traced here: 87.8 us
  Pallas kernels  84.8 us (96%)
  local copies, waits for them, and re-layouts  3.02 us (3%)
    pallas_call x1, Pallas kernels, per_device(): pl.pallas_call(functools.partial(kernel, nz, nt), out_shape=jax.ShapeDtyp...  84.8 us
    unnamed x2, local copies, waits for them, and re-layouts  3.02 us

profile of v1, /device:TPU:17, one launch (start us, length us, event | category | flops | bytes accessed | tf_op | source)
XLA Modules:
  0.0 87.8 jit_solution(11352004578750616015)
XLA Ops:
  0.0 1.4 %copy.6.extents_in = s32[6,2]{1,0:T(8,128)} copy(s32[6,2]{0,1:T(2,128)} %param.9) | data formatting | bytes 96 | tf_op args[4]
  1.4 84.8 %shard_map.55 = f32[512,128]{1,0:T(8,128)} custom-call(f32[512,128]{1,0:T(8,128)} %bitcast.5, f32[96,32,128]{2,1,0:T(8,128)} %bitcast.3, f32[6,3,31]{2,1,0:T(4,128)} %psf_in.1, s32[6]{0:T(128)} %shifts_in.1, s32[6,2]{1,0:T(8,128)} %copy.6.extents_in), custom_call_target="tpu_custom_call" | custom-call | tf_op jit(solution)/shard_map/pallas_call | solution.py:331
  86.2 1.7 %copy.8 = f32[16,32,128]{2,1,0:T(8,128)} copy(f32[16,32,128]{2,1,0:T(8,128)} %bitcast.4) | data formatting | bytes 524288

commit v2 on v1

--- a/solution.py
+++ b/solution.py
@@ -15,7 +15,7 @@
 DE, RE = D + 2 * W, R + 2 * W
 N = 8
 ORDER = (0, 24, 8, 16)
-SEMS = 2 + 10 * len(ORDER)
+SEMS = 2 + 12 * len(ORDER)
 F32, BF16 = jnp.float32, jnp.bfloat16
 
 
@@ -61,7 +61,7 @@
 
 def kernel(
     nz, nt, est, view, psf_in, shifts_in, extents_in, out,
-    raw, near, ext, zbuf, xbuf, rbuf, back, got_x, got_y, got_n,
+    raw, near, ext, zbuf, xbuf, rbuf, back, got_x, got_y, got_n, got_h,
     kz, kzt, kx, kxt, ky, kyt, psf, shifts, extents, send, recv, local,
 ):
     zs, ti = lax.axis_index("zslab"), lax.axis_index("tile")
@@ -72,11 +72,11 @@
     is_mate = mate < nz
 
     class Sent:
-        def __init__(self, number, src, dst, axis, target, exists, comes):
+        def __init__(self, number, src, dst, target, exists, comes):
             self.exists, self.comes = exists, comes
             self.copy = pltpu.make_async_remote_copy(
                 src_ref=src, dst_ref=dst, send_sem=send.at[number], recv_sem=recv.at[number],
-                device_id={axis: target}, device_id_type=MESH,
+                device_id=target, device_id_type=MESH,
             )
 
         def start(self):
@@ -85,28 +85,30 @@
         def sent(self):
             pl.when(self.exists)(self.copy.wait_send)
 
-        def arrived(self):
-            pl.when(self.comes)(self.copy.wait_recv)
+        def arrived(self, where=True):
+            pl.when(self.comes & where)(self.copy.wait_recv)
 
     is_ahead = (ahead >= 0) & (ahead < nz)
     is_behind = (behind >= 0) & (behind < nz)
     is_left, is_right = ti > 0, ti < nt - 1
+    seam = nt // 2 if nz % 2 == 0 else -1
+    seam_left, seam_right = is_left & (ti == seam), is_right & (ti == seam - 1)
+    left = {"zslab": jnp.where(seam_left, mate, zs), "tile": ti - 1}
+    right = {"zslab": jnp.where(seam_right, mate, zs), "tile": ti + 1}
     numbers = iter(range(SEMS))
 
     def to_mate(src, dst):
-        return Sent(next(numbers), src, dst, "zslab", mate, is_mate, is_mate)
-
-    def to_ahead(src, dst):
-        return Sent(next(numbers), src, dst, "zslab", ahead, is_ahead, is_behind)
-
-    def to_behind(src, dst):
-        return Sent(next(numbers), src, dst, "zslab", behind, is_behind, is_ahead)
-
-    def to_left(src, dst):
-        return Sent(next(numbers), src, dst, "tile", ti - 1, is_left, is_right)
-
-    def to_right(src, dst):
-        return Sent(next(numbers), src, dst, "tile", ti + 1, is_right, is_left)
+        return Sent(next(numbers), src, dst, {"zslab": mate}, is_mate, is_mate)
+
+    def to_ahead(src, dst, where=True):
+        return Sent(
+            next(numbers), src, dst, {"zslab": ahead}, is_ahead & where, is_behind & where
+        )
+
+    def to_behind(src, dst, where=True):
+        return Sent(
+            next(numbers), src, dst, {"zslab": behind}, is_behind & where, is_ahead & where
+        )
 
     reads = [
         pltpu.make_async_copy(src, dst, local.at[k])
@@ -120,6 +122,7 @@
     ext[...] = jnp.zeros(ext.shape, F32)
     got_x[...] = jnp.zeros(got_x.shape, F32)
     got_y[...] = jnp.zeros(got_y.shape, F32)
+    got_h[...] = jnp.zeros(got_h.shape, F32)
     near[:, 0:W] = jnp.zeros((V * D, W, C), F32)
     near[:, W + R :] = jnp.zeros((V * D, W, C), F32)
     for x in range(RE):
@@ -130,50 +133,73 @@
 
     barrier = pltpu.get_barrier_semaphore()
     beside = [
-        ("zslab", mate, is_mate), ("zslab", ahead, is_ahead), ("zslab", behind, is_behind),
-        ("tile", ti - 1, is_left), ("tile", ti + 1, is_right),
+        ({"zslab": mate}, is_mate), ({"zslab": ahead}, is_ahead), ({"zslab": behind}, is_behind),
+        ({"tile": ti - 1}, is_left), ({"tile": ti + 1}, is_right),
+        (left, seam_left), (right, seam_right),
     ]
-    for axis, target, exists in beside:
+    for target, exists in beside:
 
         @pl.when(exists)
-        def _(axis=axis, target=target):
-            pl.semaphore_signal(barrier, inc=1, device_id={axis: target}, device_id_type=MESH)
-
-    pl.semaphore_wait(barrier, sum(exists.astype(jnp.int32) for _, _, exists in beside))
+        def _(target=target):
+            pl.semaphore_signal(barrier, inc=1, device_id=target, device_id_type=MESH)
+
+    pl.semaphore_wait(barrier, sum(exists.astype(jnp.int32) for _, exists in beside))
 
     own_p, close_p, far_p = pl.ds(W, D), pl.ds(close, W), pl.ds(far, W)
 
     def rows_of(r):
         return slice(W + r, W + r + N)
 
+    def beyond(r):
+        return slice(W + R + r, W + R + r + N) if r < W else slice(r - W, r - W + N)
+
+    def crossed(where, p):
+        if p is far_p:
+            return p
+        start, other = (W, far) if p is own_p else (close, W)
+        return pl.ds(pl.multiple_of(jnp.where(where, other, start), W), W)
+
+    def to_tile(leftward, src, dst, p):
+        seam_out, seam_in = (seam_left, seam_right) if leftward else (seam_right, seam_left)
+        exists, comes = (is_left, is_right) if leftward else (is_right, is_left)
+        if p is far_p:
+            exists, comes = exists & jnp.logical_not(seam_out), comes & jnp.logical_not(seam_in)
+        return Sent(
+            next(numbers), src, dst.at[:, crossed(seam_out, p)], left if leftward else right, exists, comes
+        )
+
     def est_tile(r, p):
-        src = ext.at[rows_of(r), p]
-        if r < W:
-            return to_left(src, ext.at[W + R + r : W + R + r + N, p])
-        return to_right(src, ext.at[r - W : r - W + N, p])
+        return to_tile(r < W, ext.at[rows_of(r), p], ext.at[beyond(r)], p)
 
     def back_tile(r, p):
-        dst = got_x.at[r : r + N, p]
-        if r < W:
-            return to_right(back.at[W + R + r : W + R + r + N, p], dst)
-        return to_left(back.at[r - W : r - W + N, p], dst)
+        return to_tile(r >= W, back.at[beyond(r), p], got_x.at[r : r + N], p)
+
+    def at_seam(r):
+        return seam_right if r < W else seam_left
+
+    def by_seam(r):
+        return seam_left if r < W else seam_right
 
     views = [
-        to_left(view.at[:, 0:W], near.at[:, W + R : RE]),
-        to_right(view.at[:, R - W : R], near.at[:, 0:W]),
+        Sent(next(numbers), view.at[:, 0:W], near.at[:, W + R : RE], {"tile": ti - 1}, is_left, is_right),
+        Sent(next(numbers), view.at[:, R - W : R], near.at[:, 0:W], {"tile": ti + 1}, is_right, is_left),
     ]
     est_mate = {r: to_mate(ext.at[rows_of(r), own_p], ext.at[rows_of(r), far_p]) for r in ORDER}
     est_ahead = {r: to_ahead(ext.at[rows_of(r), close_p], ext.at[rows_of(r), far_p]) for r in ORDER}
+    est_halo = {
+        r: to_ahead(ext.at[beyond(r), close_p], ext.at[beyond(r), far_p], at_seam(r)) for r in ORDER
+    }
     est_own = {r: est_tile(r, own_p) for r in ORDER}
     est_close = {r: est_tile(r, close_p) for r in ORDER}
     est_far = {r: est_tile(r, far_p) for r in ORDER}
+    back_halo = {r: to_behind(back.at[beyond(r), far_p], got_h.at[r : r + N], at_seam(r)) for r in ORDER}
     back_far = {r: back_tile(r, far_p) for r in ORDER}
     back_close = {r: back_tile(r, close_p) for r in ORDER}
     back_own = {r: back_tile(r, own_p) for r in ORDER}
     back_behind = {r: to_behind(back.at[rows_of(r), far_p], got_y.at[r : r + N]) for r in ORDER}
     back_mate = {r: to_mate(back.at[rows_of(r), close_p], got_n.at[r : r + N]) for r in ORDER}
-    est_sends = [est_mate, est_ahead, est_own, est_close, est_far]
-    back_sends = [back_far, back_close, back_own, back_behind, back_mate]
+    est_sends = [est_mate, est_ahead, est_halo, est_own, est_close, est_far]
+    back_sends = [back_halo, back_far, back_close, back_own, back_behind, back_mate]
 
     def build():
         lane = iota((C, C), 1)
@@ -230,7 +256,7 @@
         start = W + shifts[v]
         for z in range(D):
             plane = zs * D + z
-            inside = jnp.where((plane >= extents[v, 0]) & (plane < extents[v, 1]), 1.0, 0.0)
+            inside = jnp.where((plane >= extents[0, v]) & (plane < extents[1, v]), 1.0, 0.0)
             data = near[v * D + z, pl.ds(start, R)]
             xbuf[z * R : (z + 1) * R] = inside * data / blurred[z * R : (z + 1) * R]
         o = dot(jnp.concatenate(halves(xbuf[...]), axis=1), kyt[v])
@@ -256,15 +282,15 @@
     for r in ORDER:
         est_mate[r].start()
         est_own[r].start()
-    for copy in views:
-        copy.start()
+    for copy, late in zip(views, (seam_left, seam_right)):
+        pl.when(jnp.logical_not(late))(copy.start)
     for read in reads[2:]:
         read.wait()
     build()
     depth = zs * D + iota((D, C), 0)
     count = jnp.zeros((D, C), F32)
     for v in range(V):
-        held = (depth >= extents[v, 0]) & (depth < extents[v, 1])
+        held = (depth >= extents[0, v]) & (depth < extents[1, v])
         count = count + jnp.where(held, 1.0, 0.0)
 
     for step in range(ITERS):
@@ -272,14 +298,22 @@
             est_mate[r].arrived()
             est_ahead[r].start()
             est_close[r].start()
+        if step == 0:
+            for copy, late in zip(views, (seam_left, seam_right)):
+                pl.when(late)(copy.start)
+        for r in ORDER:
+            est_own[r].arrived(at_seam(r))
+            est_halo[r].start()
         for r in ORDER:
             est_ahead[r].arrived()
             est_far[r].start()
             over(along_z, W + r, N)
         for r in ORDER:
-            for group in (est_own, est_close, est_far):
-                group[r].arrived()
-            over(along_z, W + R + r if r < W else r - W, N)
+            est_own[r].arrived(jnp.logical_not(at_seam(r)))
+            est_close[r].arrived()
+            est_far[r].arrived()
+            est_halo[r].arrived()
+            over(along_z, beyond(r).start, N)
         if step == 0:
             reads[1].wait()
             for copy in views:
@@ -289,23 +323,35 @@
             for r in ORDER:
                 group[r].sent()
         for r in ORDER:
-            over(along_z_back, W + R + r if r < W else r - W, N)
+            over(along_z_back, beyond(r).start, N)
+            back_halo[r].start()
             back_far[r].start()
-        for group in (back_close, back_own):
-            for r in ORDER:
-                group[r].start()
+        for r in ORDER:
+            pl.when(jnp.logical_not(at_seam(r)))(back_close[r].start)
+        for r in ORDER:
+            back_own[r].start()
         over(along_z_back, W, R)
+        for r in ORDER:
+
+            @pl.when(at_seam(r))
+            def _():
+                back_halo[r].arrived()
+                back[beyond(r), close_p] += got_h[r : r + N]
+                back_close[r].start()
+
         for r in ORDER:
             back_far[r].arrived()
             back[rows_of(r), far_p] += got_x[r : r + N, far_p]
             back_behind[r].start()
         for r in ORDER:
-            back_close[r].arrived()
+            back_close[r].arrived(jnp.logical_not(by_seam(r)))
+            back_own[r].arrived(by_seam(r))
             back_behind[r].arrived()
             back[rows_of(r), close_p] += got_x[r : r + N, close_p] + got_y[r : r + N]
             back_mate[r].start()
         for r in ORDER:
-            back_own[r].arrived()
+            back_own[r].arrived(jnp.logical_not(by_seam(r)))
+            back_close[r].arrived(by_seam(r))
             back_mate[r].arrived()
             for x in range(r, r + N):
                 total = back[W + x, W : W + D] + got_x[x, W : W + D] + got_n[x]
@@ -330,8 +376,8 @@
     def per_device(estimate, view_data, psf, shifts, extents):
         flat = pl.pallas_call(
             functools.partial(kernel, nz, nt),
-            out_shape=jax.ShapeDtypeStruct((D * R, C), F32),
-            in_specs=[pl.BlockSpec(memory_space=pl.ANY)] * 5,
+            out_shape=pltpu.VMEM((D * R, C), F32),
+            in_specs=[pl.BlockSpec(memory_space=pltpu.HBM)] * 5,
             out_specs=pl.BlockSpec(memory_space=pltpu.VMEM),
             scratch_shapes=[
                 pltpu.VMEM((D * R, C), F32),
@@ -344,6 +390,7 @@
                 pltpu.VMEM((R, DE, C), F32),
                 pltpu.VMEM((R, D, C), F32),
                 pltpu.VMEM((R, D, C), F32),
+                pltpu.VMEM((R, D, C), F32),
                 pltpu.VMEM((V * D, 3 * DE), BF16),
                 pltpu.VMEM((DE, 3 * C), BF16),
                 pltpu.VMEM((V, R, 3 * RE), BF16),
@@ -352,7 +399,7 @@
                 pltpu.VMEM((V, 2 * C, 2 * C), BF16),
                 pltpu.SMEM((V, 3, TAPS), F32),
                 pltpu.SMEM((V,), jnp.int32),
-                pltpu.SMEM((V, 2), jnp.int32),
+                pltpu.SMEM((2, V), jnp.int32),
                 pltpu.SemaphoreType.DMA((SEMS,)),
                 pltpu.SemaphoreType.DMA((SEMS,)),
                 pltpu.SemaphoreType.DMA((5,)),
@@ -365,7 +412,7 @@
             view_data.reshape(V * D, R, C),
             psf,
             shifts,
-            extents,
+            extents.T,
         )
         return flat.reshape(D, R, C)
 

time: 88 us -> 76.6 us (0.87)
  the two profiles are of different devices: /device:TPU:17 before, /device:TPU:20 now
where the time goes in v2:
time: 76.6 us; the launch traced here: 76.5 us
  Pallas kernels  75.8 us (99%)
    pallas_call x1, Pallas kernels, per_device(): pl.pallas_call(functools.partial(kernel, nz, nt), out_shape=pltpu.VMEM((D...  75.8 us

profile of v2, /device:TPU:20, one launch (start us, length us, event | category | flops | bytes accessed | tf_op | source)
XLA Modules:
  0.0 76.5 jit_solution(7921543163838261502)
XLA Ops:
  0.0 75.8 %shard_map.55 = f32[512,128]{1,0:T(8,128)S(1)} custom-call(f32[512,128]{1,0:T(8,128)} %bitcast.6, f32[96,32,128]{2,1,0:T(8,128)} %bitcast.5, f32[6,3,31]{2,1,0:T(4,128)} %psf_in.1, s32[6]{0:T(128)} %shifts_in.1, s32[2,6]{1,0:T(2,128)} %bitcast.7), custom_call_target="tpu_custom_call" | custom-call | tf_op jit(solution)/shard_map/pallas_call | solution.py:377
  75.8 0.7 copy.7

commit v3 on v2

--- a/solution.py
+++ b/solution.py
@@ -13,8 +13,8 @@
 W = 16
 D, R, C = 16, 32, 128
 DE, RE = D + 2 * W, R + 2 * W
-N = 8
-ORDER = (0, 24, 8, 16)
+N = 4
+ORDER = (0, 28, 4, 24, 8, 20, 12, 16)
 SEMS = 2 + 12 * len(ORDER)
 F32, BF16 = jnp.float32, jnp.bfloat16
 
@@ -125,12 +125,6 @@
     got_h[...] = jnp.zeros(got_h.shape, F32)
     near[:, 0:W] = jnp.zeros((V * D, W, C), F32)
     near[:, W + R :] = jnp.zeros((V * D, W, C), F32)
-    for x in range(RE):
-        rbuf[pl.ds(x * C + V * D, C - V * D)] = jnp.zeros((C - V * D, C), F32)
-    reads[0].wait()
-    for x in range(R):
-        ext[W + x, W : W + D] = raw[pl.ds(x, D, stride=R)]
-
     barrier = pltpu.get_barrier_semaphore()
     beside = [
         ({"zslab": mate}, is_mate), ({"zslab": ahead}, is_ahead), ({"zslab": behind}, is_behind),
@@ -143,6 +137,9 @@
         def _(target=target):
             pl.semaphore_signal(barrier, inc=1, device_id=target, device_id_type=MESH)
 
+    reads[0].wait()
+    for x in range(R):
+        ext[W + x, W : W + D] = raw[pl.ds(x, D, stride=R)]
     pl.semaphore_wait(barrier, sum(exists.astype(jnp.int32) for _, exists in beside))
 
     own_p, close_p, far_p = pl.ds(W, D), pl.ds(close, W), pl.ds(far, W)
@@ -231,10 +228,11 @@
                 mat[v, C:, C:] = jnp.zeros((C, C), BF16)
             return total + pltpu.roll(z_back, v * D, 1)
 
-        hi, lo = halves(lax.fori_loop(0, V, one, jnp.zeros((DE, C), F32)))
-        kzt[:, 0:C] = hi
-        kzt[:, C : 2 * C] = hi
-        kzt[:, 2 * C :] = lo
+        hi, lo = split_part(lax.fori_loop(0, V, one, jnp.zeros((DE, C), F32)))
+        again, low = pltpu.roll(hi, V * D, 1), pltpu.roll(lo, 2 * V * D - C, 1)
+        kzt[:, 0:C] = jnp.where(lane[0:DE] < V * D, hi, again).astype(BF16)
+        kzt[:, C : 2 * C] = jnp.where(lane[0:DE] < 2 * V * D - C, again, low).astype(BF16)
+        kzt[:, 2 * C :] = low[:, 0 : 3 * V * D - 2 * C].astype(BF16)
 
     def along_z(i, carry):
         x = 2 * i
@@ -265,12 +263,13 @@
             both = [xbuf[(i + k) * R : (i + k + 1) * R] for k in range(2)]
             o = dot(kxt[v], stacked(jnp.concatenate(both, axis=1)))
             for k in range(2):
-                rbuf[pl.ds(v * D + i + k, RE, stride=C)] = o[:, k * C : (k + 1) * C]
+                at = pl.multiple_of((v * D + i + k) * RE, RE)
+                rbuf[pl.ds(at, RE)] = o[:, k * C : (k + 1) * C]
         return carry
 
     def along_z_back(i, carry):
         x = 2 * i
-        both = [rbuf[pl.ds(pl.multiple_of((x + k) * C, C), C)] for k in range(2)]
+        both = [rbuf[pl.ds(x + k, V * D, stride=RE)] for k in range(2)]
         o = dot(kzt[...], stacked(jnp.concatenate(both, axis=1)))
         back[x] = o[:, :C]
         back[x + 1] = o[:, C:]
@@ -282,8 +281,8 @@
     for r in ORDER:
         est_mate[r].start()
         est_own[r].start()
-    for copy, late in zip(views, (seam_left, seam_right)):
-        pl.when(jnp.logical_not(late))(copy.start)
+    for copy in views:
+        copy.start()
     for read in reads[2:]:
         read.wait()
     build()
@@ -298,9 +297,6 @@
             est_mate[r].arrived()
             est_ahead[r].start()
             est_close[r].start()
-        if step == 0:
-            for copy, late in zip(views, (seam_left, seam_right)):
-                pl.when(late)(copy.start)
         for r in ORDER:
             est_own[r].arrived(at_seam(r))
             est_halo[r].start()
@@ -385,14 +381,14 @@
                 pltpu.VMEM((RE, DE, C), F32),
                 pltpu.VMEM((V, RE * D, C), F32),
                 pltpu.VMEM((D * R, C), F32),
-                pltpu.VMEM((RE * C, C), F32),
+                pltpu.VMEM((V * D * RE, C), F32),
                 pltpu.VMEM((RE, DE, C), F32),
                 pltpu.VMEM((R, DE, C), F32),
                 pltpu.VMEM((R, D, C), F32),
                 pltpu.VMEM((R, D, C), F32),
                 pltpu.VMEM((R, D, C), F32),
                 pltpu.VMEM((V * D, 3 * DE), BF16),
-                pltpu.VMEM((DE, 3 * C), BF16),
+                pltpu.VMEM((DE, 3 * V * D), BF16),
                 pltpu.VMEM((V, R, 3 * RE), BF16),
                 pltpu.VMEM((V, RE, 3 * R), BF16),
                 pltpu.VMEM((V, 2 * C, 2 * C), BF16),

time: 76.6 us -> 73.5 us (0.960)
  the two profiles are of different devices: /device:TPU:20 before, /device:TPU:236 now
where the time goes in v3:
time: 73.5 us; the launch traced here: 73.4 us
  Pallas kernels  72.7 us (99%)
    pallas_call x1, Pallas kernels, per_device(): pl.pallas_call(functools.partial(kernel, nz, nt), out_shape=pltpu.VMEM((D...  72.7 us

profile of v3, /device:TPU:236, one launch (start us, length us, event | category | flops | bytes accessed | tf_op | source)
XLA Modules:
  0.0 73.4 jit_solution(11368679839651612732)
XLA Ops:
  0.0 72.7 %shard_map.55 = f32[512,128]{1,0:T(8,128)S(1)} custom-call(f32[512,128]{1,0:T(8,128)} %bitcast.6, f32[96,32,128]{2,1,0:T(8,128)} %bitcast.5, f32[6,3,31]{2,1,0:T(4,128)} %psf_in.1, s32[6]{0:T(128)} %shifts_in.1, s32[2,6]{1,0:T(2,128)} %bitcast.7), custom_call_target="tpu_custom_call" | custom-call | tf_op jit(solution)/shard_map/pallas_call | solution.py:373
  72.7 0.7 copy.7

commit v4 on v3

--- a/solution.py
+++ b/solution.py
@@ -15,6 +15,9 @@
 DE, RE = D + 2 * W, R + 2 * W
 N = 4
 ORDER = (0, 28, 4, 24, 8, 20, 12, 16)
+GROUPS = ((0, 4), (24, 28), (8, 12), (16, 20))
+SIDES = ((0, 4, 8, 12), (16, 20, 24, 28))
+DIRECT = 2
 SEMS = 2 + 12 * len(ORDER)
 F32, BF16 = jnp.float32, jnp.bfloat16
 
@@ -67,6 +70,7 @@
     zs, ti = lax.axis_index("zslab"), lax.axis_index("tile")
     odd = lax.rem(zs, 2)
     mate, ahead, behind = zs + 1 - 2 * odd, zs + 2 - 4 * odd, zs - 2 + 4 * odd
+    other = zs - 1 + 2 * odd
     close = pl.multiple_of(2 * W * (1 - odd), W)
     far = pl.multiple_of(2 * W * odd, W)
     is_mate = mate < nz
@@ -90,6 +94,7 @@
 
     is_ahead = (ahead >= 0) & (ahead < nz)
     is_behind = (behind >= 0) & (behind < nz)
+    is_other = (other >= 0) & (other < nz)
     is_left, is_right = ti > 0, ti < nt - 1
     seam = nt // 2 if nz % 2 == 0 else -1
     seam_left, seam_right = is_left & (ti == seam), is_right & (ti == seam - 1)
@@ -99,6 +104,9 @@
 
     def to_mate(src, dst):
         return Sent(next(numbers), src, dst, {"zslab": mate}, is_mate, is_mate)
+
+    def to_other(src, dst):
+        return Sent(next(numbers), src, dst, {"zslab": other}, is_other, is_other)
 
     def to_ahead(src, dst, where=True):
         return Sent(
@@ -127,7 +135,7 @@
     near[:, W + R :] = jnp.zeros((V * D, W, C), F32)
     barrier = pltpu.get_barrier_semaphore()
     beside = [
-        ({"zslab": mate}, is_mate), ({"zslab": ahead}, is_ahead), ({"zslab": behind}, is_behind),
+        ({"zslab": mate}, is_mate), ({"zslab": other}, is_other), ({"zslab": ahead}, is_ahead), ({"zslab": behind}, is_behind),
         ({"tile": ti - 1}, is_left), ({"tile": ti + 1}, is_right),
         (left, seam_left), (right, seam_right),
     ]
@@ -182,7 +190,13 @@
         Sent(next(numbers), view.at[:, R - W : R], near.at[:, 0:W], {"tile": ti + 1}, is_right, is_left),
     ]
     est_mate = {r: to_mate(ext.at[rows_of(r), own_p], ext.at[rows_of(r), far_p]) for r in ORDER}
-    est_ahead = {r: to_ahead(ext.at[rows_of(r), close_p], ext.at[rows_of(r), far_p]) for r in ORDER}
+    est_ahead = {
+        r: to_ahead(ext.at[rows_of(r), close_p], ext.at[rows_of(r), far_p]) for r in ORDER[:-DIRECT]
+    }
+    est_direct = {
+        r: to_other(ext.at[rows_of(r), own_p], ext.at[rows_of(r), close_p]) for r in ORDER[-DIRECT:]
+    }
+    est_third = est_ahead | est_direct
     est_halo = {
         r: to_ahead(ext.at[beyond(r), close_p], ext.at[beyond(r), far_p], at_seam(r)) for r in ORDER
     }
@@ -193,10 +207,16 @@
     back_far = {r: back_tile(r, far_p) for r in ORDER}
     back_close = {r: back_tile(r, close_p) for r in ORDER}
     back_own = {r: back_tile(r, own_p) for r in ORDER}
-    back_behind = {r: to_behind(back.at[rows_of(r), far_p], got_y.at[r : r + N]) for r in ORDER}
+    back_behind = {
+        r: to_behind(back.at[rows_of(r), far_p], got_y.at[r : r + N]) for r in ORDER[DIRECT:]
+    }
+    back_direct = {
+        r: to_other(back.at[rows_of(r), far_p], got_y.at[r : r + N]) for r in ORDER[:DIRECT]
+    }
+    back_third = back_behind | back_direct
     back_mate = {r: to_mate(back.at[rows_of(r), close_p], got_n.at[r : r + N]) for r in ORDER}
-    est_sends = [est_mate, est_ahead, est_halo, est_own, est_close, est_far]
-    back_sends = [back_halo, back_far, back_close, back_own, back_behind, back_mate]
+    est_sends = [est_mate, est_third, est_halo, est_own, est_close, est_far]
+    back_sends = [back_halo, back_far, back_close, back_own, back_third, back_mate]
 
     def build():
         lane = iota((C, C), 1)
@@ -239,7 +259,7 @@
         o = dot(kz[...], stacked(jnp.concatenate([ext[x], ext[x + 1]], axis=1)))
         for v in range(V):
             for k in range(2):
-                at = pl.multiple_of((x + k) * D, D)
+                at = (x + k) * D
                 zbuf[v, pl.ds(at, D)] = o[v * D : (v + 1) * D, k * C : (k + 1) * C]
         return carry
 
@@ -247,20 +267,20 @@
         for i in range(0, D, 2):
             both = [zbuf[v, pl.ds(i + k, RE, stride=D)] for k in range(2)]
             o = dot(kx[v], stacked(jnp.concatenate(both, axis=1)))
-            xbuf[i * R : (i + 1) * R] = o[:, :C]
-            xbuf[(i + 1) * R : (i + 2) * R] = o[:, C:]
-        o = dot(jnp.concatenate(halves(xbuf[...]), axis=1), ky[v])
+            xbuf[v, i * R : (i + 1) * R] = o[:, :C]
+            xbuf[v, (i + 1) * R : (i + 2) * R] = o[:, C:]
+        o = dot(jnp.concatenate(halves(xbuf[v]), axis=1), ky[v])
         blurred = o[:, :C] + o[:, C:]
         start = W + shifts[v]
         for z in range(D):
             plane = zs * D + z
             inside = jnp.where((plane >= extents[0, v]) & (plane < extents[1, v]), 1.0, 0.0)
             data = near[v * D + z, pl.ds(start, R)]
-            xbuf[z * R : (z + 1) * R] = inside * data / blurred[z * R : (z + 1) * R]
-        o = dot(jnp.concatenate(halves(xbuf[...]), axis=1), kyt[v])
-        xbuf[...] = o[:, :C] + o[:, C:]
+            xbuf[v, z * R : (z + 1) * R] = inside * data / blurred[z * R : (z + 1) * R]
+        o = dot(jnp.concatenate(halves(xbuf[v]), axis=1), kyt[v])
+        xbuf[v] = o[:, :C] + o[:, C:]
         for i in range(0, D, 2):
-            both = [xbuf[(i + k) * R : (i + k + 1) * R] for k in range(2)]
+            both = [xbuf[v, (i + k) * R : (i + k + 1) * R] for k in range(2)]
             o = dot(kxt[v], stacked(jnp.concatenate(both, axis=1)))
             for k in range(2):
                 at = pl.multiple_of((v * D + i + k) * RE, RE)
@@ -276,11 +296,14 @@
         return carry
 
     def over(body, first, rows):
-        lax.fori_loop(first // 2, (first + rows) // 2, body, 0, unroll=2)
+        for i in range(first // 2, (first + rows) // 2):
+            body(i, 0)
 
     for r in ORDER:
         est_mate[r].start()
         est_own[r].start()
+    for copy in est_direct.values():
+        copy.start()
     for copy in views:
         copy.start()
     for read in reads[2:]:
@@ -295,33 +318,36 @@
     for step in range(ITERS):
         for r in ORDER:
             est_mate[r].arrived()
-            est_ahead[r].start()
+            if r in est_ahead:
+                est_ahead[r].start()
             est_close[r].start()
         for r in ORDER:
             est_own[r].arrived(at_seam(r))
             est_halo[r].start()
         for r in ORDER:
-            est_ahead[r].arrived()
+            est_third[r].arrived()
             est_far[r].start()
-            over(along_z, W + r, N)
-        for r in ORDER:
-            est_own[r].arrived(jnp.logical_not(at_seam(r)))
-            est_close[r].arrived()
-            est_far[r].arrived()
-            est_halo[r].arrived()
-            over(along_z, beyond(r).start, N)
+        over(along_z, W, R)
+        for side in SIDES:
+            for r in side:
+                est_own[r].arrived(jnp.logical_not(at_seam(r)))
+                est_close[r].arrived()
+                est_far[r].arrived()
+                est_halo[r].arrived()
+            over(along_z, beyond(min(side)).start, N * len(side))
         if step == 0:
             reads[1].wait()
             for copy in views:
                 copy.arrived()
-        lax.fori_loop(0, V, one_view, 0)
+        lax.fori_loop(0, V, one_view, 0, unroll=2)
         for group in est_sends:
             for r in ORDER:
                 group[r].sent()
-        for r in ORDER:
-            over(along_z_back, beyond(r).start, N)
-            back_halo[r].start()
-            back_far[r].start()
+        for group in GROUPS:
+            over(along_z_back, beyond(min(group)).start, N * len(group))
+            for r in group:
+                back_halo[r].start()
+                back_far[r].start()
         for r in ORDER:
             pl.when(jnp.logical_not(at_seam(r)))(back_close[r].start)
         for r in ORDER:
@@ -338,19 +364,26 @@
         for r in ORDER:
             back_far[r].arrived()
             back[rows_of(r), far_p] += got_x[r : r + N, far_p]
-            back_behind[r].start()
+            back_third[r].start()
         for r in ORDER:
             back_close[r].arrived(jnp.logical_not(by_seam(r)))
             back_own[r].arrived(by_seam(r))
-            back_behind[r].arrived()
-            back[rows_of(r), close_p] += got_x[r : r + N, close_p] + got_y[r : r + N]
+            if r in back_behind:
+                back_behind[r].arrived()
+                back[rows_of(r), close_p] += got_x[r : r + N, close_p] + got_y[r : r + N]
+            else:
+                back[rows_of(r), close_p] += got_x[r : r + N, close_p]
             back_mate[r].start()
         for r in ORDER:
             back_own[r].arrived(jnp.logical_not(by_seam(r)))
             back_close[r].arrived(by_seam(r))
             back_mate[r].arrived()
+            if r in back_direct:
+                back_direct[r].arrived()
             for x in range(r, r + N):
                 total = back[W + x, W : W + D] + got_x[x, W : W + D] + got_n[x]
+                if r in back_direct:
+                    total = total + got_y[x]
                 updated = ext[W + x, W : W + D] * total / count
                 if step < ITERS - 1:
                     ext[W + x, W : W + D] = updated
@@ -359,6 +392,8 @@
             if step < ITERS - 1:
                 est_mate[r].start()
                 est_own[r].start()
+                if r in est_direct:
+                    est_direct[r].start()
         for group in back_sends:
             for r in ORDER:
                 group[r].sent()
@@ -380,7 +415,7 @@
                 pltpu.VMEM((V * D, RE, C), F32),
                 pltpu.VMEM((RE, DE, C), F32),
                 pltpu.VMEM((V, RE * D, C), F32),
-                pltpu.VMEM((D * R, C), F32),
+                pltpu.VMEM((V, D * R, C), F32),
                 pltpu.VMEM((V * D * RE, C), F32),
                 pltpu.VMEM((RE, DE, C), F32),
                 pltpu.VMEM((R, DE, C), F32),

time: 73.5 us -> 70 us (0.952)
  the two profiles are of different devices: /device:TPU:236 before, /device:TPU:197 now
where the time goes in v4:
time: 70 us; the launch traced here: 69.9 us
  Pallas kernels  69.2 us (99%)
  local copies, waits for them, and re-layouts  0.71 us (1%)
    pallas_call x1, Pallas kernels, per_device(): pl.pallas_call(functools.partial(kernel, nz, nt), out_shape=pltpu.VMEM((D...  69.2 us

profile of v4, /device:TPU:197, one launch (start us, length us, event | category | flops | bytes accessed | tf_op | source)
XLA Modules:
  0.0 69.9 jit_solution(12410601048587286667)
XLA Ops:
  0.0 69.2 %shard_map.55 = f32[512,128]{1,0:T(8,128)S(1)} custom-call(f32[512,128]{1,0:T(8,128)} %bitcast.6, f32[96,32,128]{2,1,0:T(8,128)} %bitcast.5, f32[6,3,31]{2,1,0:T(4,128)} %psf_in.1, s32[6]{0:T(128)} %shifts_in.1, s32[2,6]{1,0:T(2,128)} %bitcast.7), custom_call_target="tpu_custom_call" | custom-call | tf_op jit(solution)/shard_map/pallas_call | solution.py:408
  69.2 0.7 %copy.7 = f32[16,32,128]{2,1,0:T(8,128)} copy(f32[16,32,128]{2,1,0:T(8,128)S(1)} %bitcast.4) | data formatting | bytes 524288

commit v5 on v4

--- a/solution.py
+++ b/solution.py
@@ -339,7 +339,7 @@
             reads[1].wait()
             for copy in views:
                 copy.arrived()
-        lax.fori_loop(0, V, one_view, 0, unroll=2)
+        lax.fori_loop(0, V, one_view, 0, unroll=6)
         for group in est_sends:
             for r in ORDER:
                 group[r].sent()

time: 70 us -> 69 us (0.986)
  Pallas kernels: 69.2 us -> 68.2 us
    pallas_call x1, Pallas kernels: 69.2 us -> 68.2 us  [per_device(): pl.pallas_call(functools.partial(kernel, nz, nt), out_shape=pltpu.VMEM((D...]
where the time goes in v5:
time: 69 us; the launch traced here: 68.9 us
  Pallas kernels  68.2 us (99%)
  local copies, waits for them, and re-layouts  0.71 us (1%)
    pallas_call x1, Pallas kernels, per_device(): pl.pallas_call(functools.partial(kernel, nz, nt), out_shape=pltpu.VMEM((D...  68.2 us

profile of v5, /device:TPU:197, one launch (start us, length us, event | category | flops | bytes accessed | tf_op | source)
XLA Modules:
  0.0 68.9 jit_solution(7126009005500559992)
XLA Ops:
  0.0 68.2 %shard_map.55 = f32[512,128]{1,0:T(8,128)S(1)} custom-call(f32[512,128]{1,0:T(8,128)} %bitcast.6, f32[96,32,128]{2,1,0:T(8,128)} %bitcast.5, f32[6,3,31]{2,1,0:T(4,128)} %psf_in.1, s32[6]{0:T(128)} %shifts_in.1, s32[2,6]{1,0:T(2,128)} %bitcast.7), custom_call_target="tpu_custom_call" | custom-call | tf_op jit(solution)/shard_map/pallas_call | solution.py:408
  68.2 0.7 %copy.7 = f32[16,32,128]{2,1,0:T(8,128)} copy(f32[16,32,128]{2,1,0:T(8,128)S(1)} %bitcast.4) | data formatting | bytes 524288

commit v6 on v5

--- a/solution.py
+++ b/solution.py
@@ -17,7 +17,7 @@
 ORDER = (0, 28, 4, 24, 8, 20, 12, 16)
 GROUPS = ((0, 4), (24, 28), (8, 12), (16, 20))
 SIDES = ((0, 4, 8, 12), (16, 20, 24, 28))
-DIRECT = 2
+DIRECT = 3
 SEMS = 2 + 12 * len(ORDER)
 F32, BF16 = jnp.float32, jnp.bfloat16
 

time: 69 us -> 70.8 us (1.026)
  Pallas kernels: 68.2 us -> 70 us
    pallas_call x1, Pallas kernels: 68.2 us -> 70 us  [per_device(): pl.pallas_call(functools.partial(kernel, nz, nt), out_shape=pltpu.VMEM((D...]
where the time goes in v6:
time: 70.8 us; the launch traced here: 70.7 us
  Pallas kernels  70 us (99%)
  local copies, waits for them, and re-layouts  0.71 us (1%)
    pallas_call x1, Pallas kernels, per_device(): pl.pallas_call(functools.partial(kernel, nz, nt), out_shape=pltpu.VMEM((D...  70 us

profile of v6, /device:TPU:197, one launch (start us, length us, event | category | flops | bytes accessed | tf_op | source)
XLA Modules:
  0.0 70.7 jit_solution(246989075745843258)
XLA Ops:
  0.0 70.0 %shard_map.55 = f32[512,128]{1,0:T(8,128)S(1)} custom-call(f32[512,128]{1,0:T(8,128)} %bitcast.6, f32[96,32,128]{2,1,0:T(8,128)} %bitcast.5, f32[6,3,31]{2,1,0:T(4,128)} %psf_in.1, s32[6]{0:T(128)} %shifts_in.1, s32[2,6]{1,0:T(2,128)} %bitcast.7), custom_call_target="tpu_custom_call" | custom-call | tf_op jit(solution)/shard_map/pallas_call | solution.py:408
  70.0 0.7 copy.7
